TPU v7x, 32 devices: a whole 2x2x4 slice. The times are simulated.
32 devices in a mesh: dp: 4 (over y, x), expert: 8 (over z, core).
Axes of the slice: x: 2, y: 2, z: 4, core: 2. Of those that a mesh axis runs over, the one named last changes fastest.
Arguments:
- tokens: bfloat16 [4096, 768], P(('dp', 'expert')), may hold values from -6 to 6
- cotangent: bfloat16 [4096, 768], P(('dp', 'expert')), may hold values from -6 to 6
- routes: int32 [4096, 2], P(('dp', 'expert')), may hold values from 0 to 7, all different within a row; in each aligned block of 128 rows (0 to 127, 128 to 255, ...) at most 96 rows name the same one
- gates: float32 [4096, 2], P(('dp', 'expert')), may hold values from 0.1 to 1
- w_in: bfloat16 [8, 2304, 768], P('expert', 'dp'), may hold values from -0.21875 to 0.21875
- w_out: bfloat16 [8, 2304, 768], P('expert', 'dp'), may hold values from -0.125 to 0.125
Outputs:
- d_tokens: bfloat16 [4096, 768], P(('dp', 'expert'))
- grad_in: float32 [8, 2304, 768], P('expert', 'dp')
- grad_out: float32 [8, 2304, 768], P('expert', 'dp')
Inputs may be any that keep to these rules, and one draw needn't show every extreme that they name: `routes`: within the rows of one device (128 rows) no expert is named more than 96 times, and in every draw some expert is named exactly 96 times by the rows of some device; the 2 entries of a row differ.
All inputs are finite; a program needn't handle non-finite values.
Results may differ from a plain program's by a relative error of at most 0.015.
Values may be sent and summed in bfloat16 or wider, within the bound.
A program may use at most 64 MiB of HBM per device.

v0:
```python
import jax
import jax.numpy as jnp
from jax import lax
from jax.sharding import PartitionSpec as P

tanh_coef = 0.7978845608028654
cubic_coef = 0.044715


def gelu_tanh(value):
    inner = tanh_coef * (value + cubic_coef * value * value * value)
    return 0.5 * value * (1.0 + jnp.tanh(inner))


def gelu_slope(value):
    inner = tanh_coef * (value + cubic_coef * value * value * value)
    slope_t = jnp.tanh(inner)
    return 0.5 * (1.0 + slope_t) + 0.5 * value * (1.0 - slope_t * slope_t) * tanh_coef * (
        1.0 + 3.0 * cubic_coef * value * value
    )


def dispatch_tables(route_blk, gate_blk, experts, capacity):
    tok_rows = route_blk.shape[0]
    flat = route_blk.reshape(-1)
    onehot = (flat[:, None] == jnp.arange(experts, dtype=jnp.int32)[None, :]).astype(jnp.int32)
    before = jnp.cumsum(onehot, axis=0) - onehot
    position = jnp.sum(before * onehot, axis=1)
    slots = (flat * capacity + position).reshape(tok_rows, -1)
    slot_ids = jnp.arange(experts * capacity, dtype=jnp.int32)
    placed = slot_ids[:, None, None] == slots[None, :, :]
    route_mat = jnp.sum(placed.astype(jnp.int32), axis=2).astype(jnp.bfloat16)
    gate_slot = jnp.sum(jnp.where(placed, gate_blk[None, :, :], jnp.float32(0.0)), axis=(1, 2))
    return (route_mat, gate_slot)


def shards(tokens, cotangent, routes, gates, w_in, w_out):
    experts = lax.axis_size("expert")
    tok_rows, model_width = tokens.shape
    top_count = routes.shape[1]
    capacity = 3 * tok_rows * top_count // experts
    shard_rows = w_in.shape[1]
    slot_rows = experts * capacity
    route_mat, gate_slot = dispatch_tables(routes, gates, experts, capacity)
    rows_sent = jnp.dot(route_mat, tokens, preferred_element_type=jnp.float32).astype(jnp.bfloat16)
    grad_rows = jnp.dot(route_mat, cotangent, preferred_element_type=jnp.float32)
    grads_sent = (gate_slot[:, None] * grad_rows).astype(jnp.bfloat16)
    rows_recv, grads_recv = (
        lax.all_to_all(
            rows_sent.reshape(experts, capacity, model_width),
            "expert",
            split_axis=0,
            concat_axis=0,
            tiled=True,
        ),
        lax.all_to_all(
            grads_sent.reshape(experts, capacity, model_width),
            "expert",
            split_axis=0,
            concat_axis=0,
            tiled=True,
        ),
    )
    rows_in = rows_recv.reshape(slot_rows, model_width)
    grads_in = grads_recv.reshape(slot_rows, model_width)
    piece_in = lax.all_gather(w_in[0], "dp", axis=0, tiled=True)
    piece_out = lax.all_gather(w_out[0], "dp", axis=0, tiled=True)
    pre = lax.dot_general(
        rows_in, piece_in, (((1,), (1,)), ((), ())), preferred_element_type=jnp.float32
    )
    acts = gelu_tanh(pre).astype(jnp.bfloat16)
    grad_act = lax.dot_general(
        grads_in, piece_out, (((1,), (1,)), ((), ())), preferred_element_type=jnp.float32
    )
    dpre = (grad_act * gelu_slope(pre)).astype(jnp.bfloat16)
    slot_sum = jnp.dot(dpre, piece_in, preferred_element_type=jnp.float32)
    slot_sum, acts_all, dpre_all = (slot_sum, acts, dpre)
    returned = lax.all_to_all(
        slot_sum.astype(jnp.bfloat16).reshape(experts, capacity, model_width),
        "expert",
        split_axis=0,
        concat_axis=0,
        tiled=True,
    )
    token_grads = lax.dot_general(
        route_mat,
        returned.reshape(slot_rows, model_width),
        (((0,), (0,)), ((), ())),
        preferred_element_type=jnp.float32,
    )
    d_tokens = token_grads.astype(jnp.bfloat16)
    term_in = lax.dot_general(
        dpre_all, rows_in, (((0,), (0,)), ((), ())), preferred_element_type=jnp.float32
    )
    term_out = lax.dot_general(
        acts_all, grads_in, (((0,), (0,)), ((), ())), preferred_element_type=jnp.float32
    )
    summed = lax.psum(
        jnp.concatenate([term_in, term_out], axis=1).astype(jnp.bfloat16), "dp"
    ).astype(jnp.float32)
    own_rows = lax.dynamic_slice_in_dim(summed, lax.axis_index("dp") * shard_rows, shard_rows, 0)
    grad_in = own_rows[:, :model_width][None]
    grad_out = own_rows[:, model_width:][None]
    return (d_tokens, grad_in, grad_out)


def solution(mesh):
    in_specs = (
        P(("dp", "expert"), None),
        P(("dp", "expert"), None),
        P(("dp", "expert"), None),
        P(("dp", "expert"), None),
        P("expert", "dp", None),
        P("expert", "dp", None),
    )
    out_specs = (P(("dp", "expert"), None), P("expert", "dp", None), P("expert", "dp", None))
    return jax.shard_map(shards, mesh=mesh, in_specs=in_specs, out_specs=out_specs, check_vma=False)
```

profile of v0, /device:TPU:0, one launch (start us, length us, event | category | flops | bytes accessed | tf_op | source)
XLA Modules:
  0.0 296.7 jit_solution(4136613115081568846)
XLA Ops:
  7.2 0.0 copy-start
  7.2 0.0 copy-start.2
  7.2 0.0 copy-start.1
  7.2 0.0 all-gather.7.cloned.1.call-start
  7.2 0.7 all-gather.7.cloned.1.call-update
  7.9 0.0 all-gather.5.cloned.1.call-start
  8.0 0.7 all-gather.5.cloned.1.call-update
  8.7 0.8 copy.27
  9.5 0.1 eq.43
  9.6 0.1 eq.39
  9.8 0.6 reduce-window.6
  10.4 0.2 slice_reduce_fusion
  10.6 0.1 fusion.20
  10.7 0.1 reduce_sum.30
  10.9 0.1 copy.29
  10.9 0.7 multiply_add_fusion.1
  11.6 0.1 convert_reduce_fusion
  11.7 0.0 copy-done
  11.7 1.5 convolution_convert_fusion.2
  13.2 6.3 %all-to-all-start.1 = ((bf16[8,96,768]{2,1,0:T(8,128)(2,1)}), bf16[8,96,768]{2,1,0:T(8,128)(2,1)S(1)}, u32[]{:S(2)}, u32[]{:S(2)}) async-start(bf16[8,96,768]{2,1,0:T(8,128)(2,1)} %bitcast.5), calls=%async_computation.1 | async-start | bytes 2359296 | tf_op jit(solution)/shard_map/all_to_all | solution.py:49
  19.5 0.0 copy-done.2
  19.5 0.2 select_reduce_fusion
  19.7 0.0 copy-done.1
  19.7 1.5 multiply_convert_fusion.2
  21.2 27.7 %all-to-all-done.1 = bf16[8,96,768]{2,1,0:T(8,128)(2,1)S(1)} async-done(((bf16[8,96,768]{2,1,0:T(8,128)(2,1)}), bf16[8,96,768]{2,1,0:T(8,128)(2,1)S(1)}, u32[]{:S(2)}, u32[]{:S(2)}) %all-to-all-start.1) | async-done | bytes 1179680 | tf_op jit(solution)/shard_map/all_to_all | solution.py:49
  48.9 3.6 %all-to-all-start = ((bf16[8,96,768]{2,1,0:T(8,128)(2,1)}), bf16[8,96,768]{2,1,0:T(8,128)(2,1)S(1)}, u32[]{:S(2)}, u32[]{:S(2)}) async-start(bf16[8,96,768]{2,1,0:T(8,128)(2,1)} %bitcast.2), calls=%async_computation | async-start | bytes 2359296 | tf_op jit(solution)/shard_map/all_to_all | solution.py:56
  52.5 0.0 all-reduce.2.cloned.1.call-start
  52.6 7.3 %all-gather.7.cloned.1.call-done = bf16[1,2304,768]{2,1,0:T(8,128)(2,1)} async-done(((bf16[1,576,768]{2,1,0:T(8,128)(2,1)}), bf16[1,2304,768]{2,1,0:T(8,128)(2,1)}) %all-gather.7.cloned.1.call-update) | async-done | bytes 3538960 | tf_op jit(solution)/shard_map/all_gather | solution.py:66
  59.9 7.0 %fusion.9 = f32[768,2304]{1,0:T(8,128)} fusion(bf16[768,768]{1,0:T(8,128)(2,1)S(1)} %bitcast.38, bf16[1,2304,768]{2,1,0:T(8,128)(2,1)} %all-gather.7.cloned.1.call-done), kind=kOutput, calls=%fused_computation.15 | convolution fusion | flops 2717908992 | bytes 11796480 | tf_op jit(solution)/shard_map/dot_general | solution.py:68
  66.8 15.0 %all-to-all-done = bf16[8,96,768]{2,1,0:T(8,128)(2,1)S(1)} async-done(((bf16[8,96,768]{2,1,0:T(8,128)(2,1)}), bf16[8,96,768]{2,1,0:T(8,128)(2,1)S(1)}, u32[]{:S(2)}, u32[]{:S(2)}) %all-to-all-start) | async-done | bytes 1179680 | tf_op jit(solution)/shard_map/all_to_all | solution.py:56
  81.8 8.2 %convolution_convert_fusion = bf16[2304,768]{0,1:T(8,128)(2,1)} fusion(bf16[768,768]{1,0:T(8,128)(2,1)S(1)} %bitcast.40, f32[768,2304]{1,0:T(8,128)} %fusion.9), kind=kOutput, calls=%fused_computation.11 | convolution fusion | flops 2735603712 | bytes 11796480 | tf_op jit(solution)/shard_map/dot_general | solution.py:95
  90.1 18.9 %all-gather.5.cloned.1.call-done = bf16[1,2304,768]{2,1,0:T(8,128)(2,1)} async-done(((bf16[1,576,768]{2,1,0:T(8,128)(2,1)}), bf16[1,2304,768]{2,1,0:T(8,128)(2,1)}) %all-gather.5.cloned.1.call-update) | async-done | bytes 3538960 | tf_op jit(solution)/shard_map/all_gather | solution.py:67
  109.0 8.4 %fusion.6 = bf16[768,2304]{1,0:T(8,128)(2,1)S(1)} fusion(f32[768,2304]{1,0:T(8,128)} %fusion.9, bf16[768,768]{1,0:T(8,128)(2,1)S(1)} %bitcast.41, bf16[1,2304,768]{2,1,0:T(8,128)(2,1)} %all-gather.5.cloned.1.call-done), kind=kOutput, calls=%fused_computation.8 | convolution fusion | flops 2751528960 | bytes 15335424 | tf_op jit(solution)/shard_map/dot_general | solution.py:72
  117.4 0.0 copy-start.3
  117.4 1.7 copy-done.3
  119.1 4.7 %convolution_convert_fusion.1 = bf16[2304,768]{0,1:T(8,128)(2,1)} fusion(bf16[768,2304]{1,0:T(8,128)(2,1)S(1)} %fusion.6, bf16[768,768]{1,0:T(8,128)(2,1)S(1)} %bitcast.39), kind=kOutput, calls=%fused_computation.12 | convolution fusion | flops 2719678464 | bytes 8257536 | tf_op jit(solution)/shard_map/dot_general | solution.py:92
  123.8 6.4 %pad_maximum_fusion = bf16[2304,1536]{0,1:T(8,128)(2,1)} fusion(bf16[2304,768]{0,1:T(8,128)(2,1)} %convolution_convert_fusion, bf16[2304,768]{0,1:T(8,128)(2,1)} %convolution_convert_fusion.1), kind=kLoop, calls=%fused_computation.9 | loop fusion | flops 14155776 | bytes 14155776 | tf_op jit(solution)/shard_map/concatenate | solution.py:99
  130.2 0.0 all-reduce.2.cloned.1.call-update
  130.3 7.0 %fusion.16 = bf16[768,768]{1,0:T(8,128)(2,1)} fusion(bf16[768,2304]{1,0:T(8,128)(2,1)} %copy-done.3, bf16[1,2304,768]{2,1,0:T(8,128)(2,1)} %all-gather.7.cloned.1.call-done), kind=kOutput, calls=%fused_computation.26 | convolution fusion | flops 2718498816 | bytes 8257536 | tf_op jit(solution)/shard_map/dot_general | solution.py:76
  137.3 4.6 %all-to-all-start.2 = ((bf16[8,96,768]{2,1,0:T(8,128)(2,1)}), bf16[8,96,768]{2,1,0:T(8,128)(2,1)S(1)}, u32[]{:S(2)}, u32[]{:S(2)}) async-start(bf16[8,96,768]{2,1,0:T(8,128)(2,1)} %bitcast.8), calls=%async_computation.2 | async-start | bytes 2359296 | tf_op jit(solution)/shard_map/all_to_all | solution.py:78
  141.8 29.4 %all-to-all-done.2 = bf16[8,96,768]{2,1,0:T(8,128)(2,1)S(1)} async-done(((bf16[8,96,768]{2,1,0:T(8,128)(2,1)}), bf16[8,96,768]{2,1,0:T(8,128)(2,1)S(1)}, u32[]{:S(2)}, u32[]{:S(2)}) %all-to-all-start.2) | async-done | bytes 1179680 | tf_op jit(solution)/shard_map/all_to_all | solution.py:78
  171.2 1.0 convolution_convert_fusion.3
  172.3 109.5 %all-reduce.2.cloned.1.call-done = bf16[2304,1536]{0,1:T(8,128)(2,1)} async-done(((bf16[2304,1536]{0,1:T(8,128)(2,1)}), bf16[2304,1536]{0,1:T(8,128)(2,1)}) %all-reduce.2.cloned.1.call-update) | async-done | bytes 7077904 | tf_op jit(solution)/shard_map/psum | solution.py:98
  281.8 2.4 dynamic-slice_convert_fusion
  284.2 1.5 slice_bitcast_fusion
  285.8 2.8 copy.30
  288.5 1.7 copy.31
  (3 shorter events, 0.0 us)
Async XLA Ops:
  7.2 4.6 %copy-start = (bf16[128,768]{1,0:T(8,128)(2,1)S(1)}, bf16[128,768]{1,0:T(8,128)(2,1)}, u32[]{:S(2)}) copy-start(bf16[128,768]{1,0:T(8,128)(2,1)} %param.6) | copy-start | bytes 589828
  7.2 12.3 %copy-start.2 = (f32[128,2]{0,1:T(2,128)S(1)}, f32[128,2]{0,1:T(2,128)}, u32[]{:S(2)}) copy-start(f32[128,2]{0,1:T(2,128)} %param.9) | copy-start | bytes 3076
  7.2 12.5 %copy-start.1 = (bf16[128,768]{1,0:T(8,128)(2,1)S(1)}, bf16[128,768]{1,0:T(8,128)(2,1)}, u32[]{:S(2)}) copy-start(bf16[128,768]{1,0:T(8,128)(2,1)} %param.7) | copy-start | bytes 589828
  7.2 52.7 %all-gather.7.cloned.1.call-start = ((), (), s32[]{:S(2)}) async-start(), calls=%async_computation.5 | async-start | bytes 4423680 | tf_op jit(solution)/shard_map/all_gather | solution.py:66
  7.9 101.1 %all-gather.5.cloned.1.call-start = ((), (), s32[]{:S(2)}) async-start(), calls=%async_computation.4 | async-start | bytes 4423680 | tf_op jit(solution)/shard_map/all_gather | solution.py:67
  13.2 35.7 %all-to-all-start.1 = ((bf16[8,96,768]{2,1,0:T(8,128)(2,1)}), bf16[8,96,768]{2,1,0:T(8,128)(2,1)S(1)}, u32[]{:S(2)}, u32[]{:S(2)}) async-start(bf16[8,96,768]{2,1,0:T(8,128)(2,1)} %bitcast.5), calls=%async_computation.1 | async-start | bytes 2359296 | tf_op jit(solution)/shard_map/all_to_all | solution.py:49
  48.9 32.9 %all-to-all-start = ((bf16[8,96,768]{2,1,0:T(8,128)(2,1)}), bf16[8,96,768]{2,1,0:T(8,128)(2,1)S(1)}, u32[]{:S(2)}, u32[]{:S(2)}) async-start(bf16[8,96,768]{2,1,0:T(8,128)(2,1)} %bitcast.2), calls=%async_computation | async-start | bytes 2359296 | tf_op jit(solution)/shard_map/all_to_all | solution.py:56
  52.5 229.3 %all-reduce.2.cloned.1.call-start = ((), (), s32[]{:S(2)}) async-start(), calls=%async_computation.3 | async-start | bytes 14155776 | tf_op jit(solution)/shard_map/psum | solution.py:98
  117.4 1.8 copy-start.3
  137.3 34.0 %all-to-all-start.2 = ((bf16[8,96,768]{2,1,0:T(8,128)(2,1)}), bf16[8,96,768]{2,1,0:T(8,128)(2,1)S(1)}, u32[]{:S(2)}, u32[]{:S(2)}) async-start(bf16[8,96,768]{2,1,0:T(8,128)(2,1)} %bitcast.8), calls=%async_computation.2 | async-start | bytes 2359296 | tf_op jit(solution)/shard_map/all_to_all | solution.py:78
Sparse Core Ops, SparseCore 0:
  9.9 49.9 all-gather.6
  61.7 47.2 all-gather.4
  130.4 151.3 all-reduce.1
where the time goes:
time: 297 us
  waiting for transfers between devices  209 us (70%)
  matrix products  39.2 us (13%)
  starting transfers between devices  14.6 us (5%)
  between operations  13.9 us (5%)
  other arithmetic  10.5 us (4%)
  local copies, waits for them, and re-layouts  9.23 us (3%)
    psum x1, waiting for transfers between devices, shards(): lax.psum(jnp.concatenate([term_in, term_out], axis=1).astype(jnp.bfloat16...  110 us
    all_to_all x1, waiting for transfers between devices, shards(): lax.all_to_all(slot_sum.astype(jnp.bfloat16).reshape(experts, capacity, m...  29.4 us
    all_to_all x1, waiting for transfers between devices, shards(): lax.all_to_all(rows_sent.reshape(experts, capacity, model_width), 'expert...  27.7 us
    all_gather x1, waiting for transfers between devices, shards(): piece_out = lax.all_gather(w_out[0], 'dp', axis=0, tiled=True)  18.9 us
    all_to_all x1, waiting for transfers between devices, shards(): lax.all_to_all(grads_sent.reshape(experts, capacity, model_width), 'exper...  15 us
    dot_general x1, matrix products, shards(): lax.dot_general(grads_in, piece_out, (((1,), (1,)), ((), ())), preferred_...  8.36 us
    dot_general x1, matrix products, shards(): lax.dot_general(acts_all, grads_in, (((0,), (0,)), ((), ())), preferred_e...  8.23 us
    all_gather x1, waiting for transfers between devices, shards(): piece_in = lax.all_gather(w_in[0], 'dp', axis=0, tiled=True)  7.31 us
  transfers between devices with their start and end apart: 6, of which 6 were waited for; matrix products, arithmetic and copies ran while one was open for 10% of the time, Pallas kernels for 0%

commit v1 on v0

--- a/solution.py
+++ b/solution.py
@@ -32,6 +32,23 @@
     route_mat = jnp.sum(placed.astype(jnp.int32), axis=2).astype(jnp.bfloat16)
     gate_slot = jnp.sum(jnp.where(placed, gate_blk[None, :, :], jnp.float32(0.0)), axis=(1, 2))
     return (route_mat, gate_slot)
+
+
+def exchange_sum(term, shard_rows):
+    size = lax.axis_size("dp")
+    me = lax.axis_index("dp")
+
+    def piece(owner):
+        return lax.dynamic_slice_in_dim(term, owner * shard_rows, shard_rows, 0)
+
+    received = [
+        lax.ppermute(piece(me ^ step), "dp", [(src, src ^ step) for src in range(size)])
+        for step in range(1, size)
+    ]
+    total = piece(me).astype(jnp.float32)
+    for block in received:
+        total = total + block.astype(jnp.float32)
+    return total
 
 
 def shards(tokens, cotangent, routes, gates, w_in, w_out):
@@ -95,12 +112,8 @@
     term_out = lax.dot_general(
         acts_all, grads_in, (((0,), (0,)), ((), ())), preferred_element_type=jnp.float32
     )
-    summed = lax.psum(
-        jnp.concatenate([term_in, term_out], axis=1).astype(jnp.bfloat16), "dp"
-    ).astype(jnp.float32)
-    own_rows = lax.dynamic_slice_in_dim(summed, lax.axis_index("dp") * shard_rows, shard_rows, 0)
-    grad_in = own_rows[:, :model_width][None]
-    grad_out = own_rows[:, model_width:][None]
+    grad_out = exchange_sum(term_out.astype(jnp.bfloat16), shard_rows)[None]
+    grad_in = exchange_sum(term_in.astype(jnp.bfloat16), shard_rows)[None]
     return (d_tokens, grad_in, grad_out)
 
 

time: 297 us -> 216 us (0.73)
  waiting for transfers between devices: 209 us -> 129 us
  starting transfers between devices: 14.6 us -> 22.4 us
  local copies, waits for them, and re-layouts: 9.23 us -> 5.01 us
  matrix products: 39.2 us -> 35.4 us
    psum x1 -> x0, waiting for transfers between devices: 110 us -> none  [shards(): lax.psum(jnp.concatenate([term_in, term_out], axis=1).astype(jnp.bfloat16...]
    ppermute x0 -> x6, waiting for transfers between devices: none -> 59.6 us  [exchange_sum(): lax.ppermute(piece(me ^ step), 'dp', [(src, src ^ step) for src in range(...]
    all_to_all x1, waiting for transfers between devices: 29.4 us -> 0.01 us  [shards(): lax.all_to_all(slot_sum.astype(jnp.bfloat16).reshape(experts, capacity, m...]
    ppermute x0 -> x6, starting transfers between devices: none -> 7.87 us  [exchange_sum(): lax.ppermute(piece(me ^ step), 'dp', [(src, src ^ step) for src in range(...]
    broadcast_in_dim x0 -> x2, other arithmetic: none -> 7.15 us  [the longest x1 3.58 us: shards(): grad_in = exchange_sum(term_in.astype(jnp.bfloat16), shard_rows)[None]]
    concatenate x1 -> x0, other arithmetic: 6.45 us -> none  [shards(): jnp.concatenate([term_in, term_out], axis=1).astype(jnp.bfloat16)]
    unnamed x11 -> x13, local copies, waits for them, and re-layouts: 7 us -> 2.49 us
    dot_general x1, matrix products: 7 us -> 3.94 us  [shards(): slot_sum = jnp.dot(dpre, piece_in, preferred_element_type=jnp.float32)]
  transfers between devices with their start and end apart: 6 -> 11, of which waited for: 6 -> 9; matrix products, arithmetic and copies ran while one was open for 10% -> 15% of each run, Pallas kernels for 0% -> 0%
where the time goes in v1:
time: 216 us; the launch traced here: 215 us
  waiting for transfers between devices  129 us (60%)
  matrix products  35.4 us (16%)
  starting transfers between devices  22.4 us (10%)
  between operations  14.2 us (7%)
  other arithmetic  8.85 us (4%)
  local copies, waits for them, and re-layouts  5.01 us (2%)
    ppermute x6, waiting for transfers between devices, exchange_sum(): lax.ppermute(piece(me ^ step), 'dp', [(src, src ^ step) for src in range(...  59.6 us
    all_to_all x1, waiting for transfers between devices, shards(): lax.all_to_all(rows_sent.reshape(experts, capacity, model_width), 'expert...  27.7 us
    all_gather x1, waiting for transfers between devices, shards(): piece_out = lax.all_gather(w_out[0], 'dp', axis=0, tiled=True)  18.2 us
    all_to_all x1, waiting for transfers between devices, shards(): lax.all_to_all(grads_sent.reshape(experts, capacity, model_width), 'exper...  15 us
    dot_general x1, matrix products, shards(): lax.dot_general(acts_all, grads_in, (((0,), (0,)), ((), ())), preferred_e...  8.93 us
    dot_general x1, matrix products, shards(): lax.dot_general(grads_in, piece_out, (((1,), (1,)), ((), ())), preferred_...  8.36 us
    ppermute x6, starting transfers between devices, exchange_sum(): lax.ppermute(piece(me ^ step), 'dp', [(src, src ^ step) for src in range(...  7.87 us
    all_gather x1, waiting for transfers between devices, shards(): piece_in = lax.all_gather(w_in[0], 'dp', axis=0, tiled=True)  7.33 us
  transfers between devices with their start and end apart: 11, of which 9 were waited for; matrix products, arithmetic and copies ran while one was open for 15% of the time, Pallas kernels for 0%

profile of v1, /device:TPU:0, one launch (start us, length us, event | category | flops | bytes accessed | tf_op | source)
XLA Modules:
  0.0 215.2 jit_solution(9012103263357388384)
XLA Ops:
  7.2 0.0 copy-start
  7.2 0.0 copy-start.4
  7.2 0.0 copy-start.3
  7.2 0.0 all-gather.7.cloned.1.call-start
  7.2 0.7 all-gather.7.cloned.1.call-update
  7.9 0.0 all-gather.5.cloned.1.call-start
  8.0 0.7 all-gather.5.cloned.1.call-update
  8.7 0.8 copy.21
  9.5 0.1 eq.43
  9.6 0.1 eq.39
  9.8 0.6 reduce-window.6
  10.4 0.2 slice_reduce_fusion
  10.6 0.1 fusion.20
  10.7 0.1 reduce_sum.30
  10.9 0.1 copy.23
  10.9 0.7 multiply_add_fusion.1
  11.6 0.1 convert_reduce_fusion
  11.7 0.0 copy-done
  11.7 1.5 convolution_convert_fusion.2
  13.2 6.3 %all-to-all-start.1 = ((bf16[8,96,768]{2,1,0:T(8,128)(2,1)}), bf16[8,96,768]{2,1,0:T(8,128)(2,1)S(1)}, u32[]{:S(2)}, u32[]{:S(2)}) async-start(bf16[8,96,768]{2,1,0:T(8,128)(2,1)} %bitcast.5), calls=%async_computation.1 | async-start | bytes 2359296 | tf_op jit(solution)/shard_map/all_to_all | solution.py:66
  19.5 0.0 copy-done.4
  19.5 0.2 select_reduce_fusion
  19.7 0.0 copy-done.3
  19.7 1.5 multiply_convert_fusion.2
  21.2 27.7 %all-to-all-done.1 = bf16[8,96,768]{2,1,0:T(8,128)(2,1)S(1)} async-done(((bf16[8,96,768]{2,1,0:T(8,128)(2,1)}), bf16[8,96,768]{2,1,0:T(8,128)(2,1)S(1)}, u32[]{:S(2)}, u32[]{:S(2)}) %all-to-all-start.1) | async-done | bytes 1179680 | tf_op jit(solution)/shard_map/all_to_all | solution.py:66
  48.9 3.6 %all-to-all-start = ((bf16[8,96,768]{2,1,0:T(8,128)(2,1)}), bf16[8,96,768]{2,1,0:T(8,128)(2,1)S(1)}, u32[]{:S(2)}, u32[]{:S(2)}) async-start(bf16[8,96,768]{2,1,0:T(8,128)(2,1)} %bitcast.2), calls=%async_computation | async-start | bytes 2359296 | tf_op jit(solution)/shard_map/all_to_all | solution.py:73
  52.5 7.3 %all-gather.7.cloned.1.call-done = bf16[1,2304,768]{2,1,0:T(8,128)(2,1)} async-done(((bf16[1,576,768]{2,1,0:T(8,128)(2,1)}), bf16[1,2304,768]{2,1,0:T(8,128)(2,1)}) %all-gather.7.cloned.1.call-update) | async-done | bytes 3538960 | tf_op jit(solution)/shard_map/all_gather | solution.py:83
  59.9 7.0 %fusion.9 = f32[768,2304]{1,0:T(8,128)} fusion(bf16[768,768]{1,0:T(8,128)(2,1)S(1)} %bitcast.38, bf16[1,2304,768]{2,1,0:T(8,128)(2,1)} %all-gather.7.cloned.1.call-done), kind=kOutput, calls=%fused_computation.14 | convolution fusion | flops 2717908992 | bytes 11796480 | tf_op jit(solution)/shard_map/dot_general | solution.py:85
  66.8 15.0 %all-to-all-done = bf16[8,96,768]{2,1,0:T(8,128)(2,1)S(1)} async-done(((bf16[8,96,768]{2,1,0:T(8,128)(2,1)}), bf16[8,96,768]{2,1,0:T(8,128)(2,1)S(1)}, u32[]{:S(2)}, u32[]{:S(2)}) %all-to-all-start) | async-done | bytes 1179680 | tf_op jit(solution)/shard_map/all_to_all | solution.py:73
  81.8 8.9 %convolution_convert_fusion = bf16[2304,768]{1,0:T(8,128)(2,1)} fusion(bf16[768,768]{1,0:T(8,128)(2,1)S(1)} %bitcast.40, f32[768,2304]{1,0:T(8,128)} %fusion.9), kind=kOutput, calls=%fused_computation.10 | convolution fusion | flops 2735603712 | bytes 11796480 | tf_op jit(solution)/shard_map/dot_general | solution.py:112
  90.8 18.2 %all-gather.5.cloned.1.call-done = bf16[1,2304,768]{2,1,0:T(8,128)(2,1)} async-done(((bf16[1,576,768]{2,1,0:T(8,128)(2,1)}), bf16[1,2304,768]{2,1,0:T(8,128)(2,1)}) %all-gather.5.cloned.1.call-update) | async-done | bytes 3538960 | tf_op jit(solution)/shard_map/all_gather | solution.py:84
  109.0 8.4 %fusion.6 = bf16[768,2304]{1,0:T(8,128)(2,1)S(1)} fusion(f32[768,2304]{1,0:T(8,128)} %fusion.9, bf16[768,768]{1,0:T(8,128)(2,1)S(1)} %bitcast.41, bf16[1,2304,768]{2,1,0:T(8,128)(2,1)} %all-gather.5.cloned.1.call-done), kind=kOutput, calls=%fused_computation.8 | convolution fusion | flops 2751528960 | bytes 15335424 | tf_op jit(solution)/shard_map/dot_general | solution.py:89
  117.4 0.0 copy-start.1
  117.4 3.2 %convolution_convert_fusion.1 = bf16[2304,768]{1,0:T(8,128)(2,1)S(1)} fusion(bf16[768,2304]{1,0:T(8,128)(2,1)S(1)} %fusion.6, bf16[768,768]{1,0:T(8,128)(2,1)S(1)} %bitcast.39), kind=kOutput, calls=%fused_computation.11 | convolution fusion | flops 2719678464 | bytes 8257536 | tf_op jit(solution)/shard_map/dot_general | solution.py:109
  120.6 0.0 copy-done.1
  120.6 0.0 copy-start.2
  120.6 0.0 copy-start.5
  120.7 1.8 constant_dynamic-slice_fusion.2
  122.5 1.7 copy-done.2
  124.2 1.5 collective-permute-start.2
  125.6 0.0 copy-done.5
  125.6 3.9 %fusion.16 = bf16[768,768]{1,0:T(8,128)(2,1)} fusion(bf16[768,2304]{1,0:T(8,128)(2,1)S(1)} %fusion.6, bf16[1,2304,768]{2,1,0:T(8,128)(2,1)S(1)} %copy-done.5), kind=kOutput, calls=%fused_computation.24 | convolution fusion | flops 2718498816 | bytes 8257536 | tf_op jit(solution)/shard_map/dot_general | solution.py:93
  129.6 4.6 %all-to-all-start.2 = ((bf16[8,96,768]{2,1,0:T(8,128)(2,1)}), bf16[8,96,768]{2,1,0:T(8,128)(2,1)S(1)}, u32[]{:S(2)}, u32[]{:S(2)}) async-start(bf16[8,96,768]{2,1,0:T(8,128)(2,1)} %bitcast.8), calls=%async_computation.2 | async-start | bytes 2359296 | tf_op jit(solution)/shard_map/all_to_all | solution.py:95
  134.1 1.5 collective-permute-start.1
  135.6 0.6 collective-permute-start
  136.2 1.4 collective-permute-start.5
  137.6 1.5 collective-permute-start.4
  139.1 8.9 %collective-permute-done.2 = bf16[576,768]{1,0:T(8,128)(2,1)} collective-permute-done((bf16[576,768]{1,0:T(8,128)(2,1)}, bf16[576,768]{1,0:T(8,128)(2,1)}, u32[]{:S(2)}, u32[]{:S(2)}) %collective-permute-start.2) | collective-permute-done | bytes 884768 | tf_op jit(solution)/shard_map/ppermute | solution.py:45
  148.0 1.5 collective-permute-start.3
  149.4 17.5 %collective-permute-done.1 = bf16[576,768]{1,0:T(8,128)(2,1)} collective-permute-done((bf16[576,768]{1,0:T(8,128)(2,1)}, bf16[576,768]{1,0:T(8,128)(2,1)}, u32[]{:S(2)}, u32[]{:S(2)}) %collective-permute-start.1) | collective-permute-done | bytes 884768 | tf_op jit(solution)/shard_map/ppermute | solution.py:45
  166.9 0.0 collective-permute-done
  166.9 3.6 %add_bitcast_fusion.1 = f32[1,576,768]{2,1,0:T(8,128)} fusion(bf16[576,768]{1,0:T(8,128)(2,1)} %collective-permute-done.2, bf16[576,768]{1,0:T(8,128)(2,1)} %collective-permute-done.1, bf16[576,768]{1,0:T(8,128)(2,1)} %collective-permute-done, bf16[2304,768]{1,0:T(8,128)(2,1)} %copy-done.2, s32[]{:T(128)S(6)} %select_n.21), kind=kLoop, calls=%fused_computation.23 | loop fusion | flops 3096576 | bytes 5308420 | tf_op jit(solution)/shard_map/broadcast_in_dim | solution.py:116
  170.5 15.4 %collective-permute-done.5 = bf16[576,768]{1,0:T(8,128)(2,1)} collective-permute-done((bf16[576,768]{1,0:T(8,128)(2,1)}, bf16[576,768]{1,0:T(8,128)(2,1)}, u32[]{:S(2)}, u32[]{:S(2)}) %collective-permute-start.5) | collective-permute-done | bytes 884768 | tf_op jit(solution)/shard_map/ppermute | solution.py:45
  185.9 17.7 %collective-permute-done.4 = bf16[576,768]{1,0:T(8,128)(2,1)} collective-permute-done((bf16[576,768]{1,0:T(8,128)(2,1)S(1)}, bf16[576,768]{1,0:T(8,128)(2,1)}, u32[]{:S(2)}, u32[]{:S(2)}) %collective-permute-start.4) | collective-permute-done | bytes 884768 | tf_op jit(solution)/shard_map/ppermute | solution.py:45
  203.6 0.1 collective-permute-done.3
  203.7 3.6 %add_bitcast_fusion = f32[1,576,768]{2,1,0:T(8,128)} fusion(bf16[576,768]{1,0:T(8,128)(2,1)} %collective-permute-done.5, bf16[576,768]{1,0:T(8,128)(2,1)} %collective-permute-done.4, bf16[576,768]{1,0:T(8,128)(2,1)} %collective-permute-done.3, bf16[2304,768]{1,0:T(8,128)(2,1)} %convolution_convert_fusion, s32[]{:T(128)S(6)} %select_n.21), kind=kLoop, calls=%fused_computation.22 | loop fusion | flops 3096576 | bytes 5308420 | tf_op jit(solution)/shard_map/broadcast_in_dim | solution.py:115
  207.3 0.0 all-to-all-done.2
  207.3 1.0 convolution_convert_fusion.3
  (3 shorter events, 0.0 us)
Async XLA Ops:
  7.2 4.6 %copy-start = (bf16[128,768]{1,0:T(8,128)(2,1)S(1)}, bf16[128,768]{1,0:T(8,128)(2,1)}, u32[]{:S(2)}) copy-start(bf16[128,768]{1,0:T(8,128)(2,1)} %param.6) | copy-start | bytes 589828
  7.2 12.3 %copy-start.4 = (f32[128,2]{0,1:T(2,128)S(1)}, f32[128,2]{0,1:T(2,128)}, u32[]{:S(2)}) copy-start(f32[128,2]{0,1:T(2,128)} %param.9) | copy-start | bytes 3076
  7.2 12.5 %copy-start.3 = (bf16[128,768]{1,0:T(8,128)(2,1)S(1)}, bf16[128,768]{1,0:T(8,128)(2,1)}, u32[]{:S(2)}) copy-start(bf16[128,768]{1,0:T(8,128)(2,1)} %param.7) | copy-start | bytes 589828
  7.2 52.7 %all-gather.7.cloned.1.call-start = ((), (), s32[]{:S(2)}) async-start(), calls=%async_computation.4 | async-start | bytes 4423680 | tf_op jit(solution)/shard_map/all_gather | solution.py:83
  7.9 101.1 %all-gather.5.cloned.1.call-start = ((), (), s32[]{:S(2)}) async-start(), calls=%async_computation.3 | async-start | bytes 4423680 | tf_op jit(solution)/shard_map/all_gather | solution.py:84
  13.2 35.7 %all-to-all-start.1 = ((bf16[8,96,768]{2,1,0:T(8,128)(2,1)}), bf16[8,96,768]{2,1,0:T(8,128)(2,1)S(1)}, u32[]{:S(2)}, u32[]{:S(2)}) async-start(bf16[8,96,768]{2,1,0:T(8,128)(2,1)} %bitcast.5), calls=%async_computation.1 | async-start | bytes 2359296 | tf_op jit(solution)/shard_map/all_to_all | solution.py:66
  48.9 32.9 %all-to-all-start = ((bf16[8,96,768]{2,1,0:T(8,128)(2,1)}), bf16[8,96,768]{2,1,0:T(8,128)(2,1)S(1)}, u32[]{:S(2)}, u32[]{:S(2)}) async-start(bf16[8,96,768]{2,1,0:T(8,128)(2,1)} %bitcast.2), calls=%async_computation | async-start | bytes 2359296 | tf_op jit(solution)/shard_map/all_to_all | solution.py:73
  117.4 3.3 %copy-start.1 = (bf16[2304,768]{1,0:T(8,128)(2,1)S(1)}, bf16[2304,768]{1,0:T(8,128)(2,1)}, u32[]{:S(2)}) copy-start(bf16[2304,768]{1,0:T(8,128)(2,1)} %convolution_convert_fusion) | copy-start | bytes 10616836
  120.6 3.5 %copy-start.2 = (bf16[2304,768]{1,0:T(8,128)(2,1)}, bf16[2304,768]{1,0:T(8,128)(2,1)S(1)}, u32[]{:S(2)}) copy-start(bf16[2304,768]{1,0:T(8,128)(2,1)S(1)} %convolution_convert_fusion.1) | copy-start | bytes 10616836
  120.6 5.0 %copy-start.5 = (bf16[1,2304,768]{2,1,0:T(8,128)(2,1)S(1)}, bf16[1,2304,768]{2,1,0:T(8,128)(2,1)}, u32[]{:S(2)}) copy-start(bf16[1,2304,768]{2,1,0:T(8,128)(2,1)} %all-gather.7.cloned.1.call-done) | copy-start | bytes 10616836
  124.2 23.8 %collective-permute-start.2 = (bf16[576,768]{1,0:T(8,128)(2,1)}, bf16[576,768]{1,0:T(8,128)(2,1)}, u32[]{:S(2)}, u32[]{:S(2)}) collective-permute-start(bf16[576,768]{1,0:T(8,128)(2,1)} %get-tuple-element.10), channel_id=1, source_target_pairs={{0,24},{8,16},{16,8},{24,0},{1,25},{9,17},{17,9},{25,1},{2,26},{10... | collective-permute-start | bytes 2654216 | tf_op jit(solution)/shard_map/ppermute | solution.py:45
  129.6 77.7 %all-to-all-start.2 = ((bf16[8,96,768]{2,1,0:T(8,128)(2,1)}), bf16[8,96,768]{2,1,0:T(8,128)(2,1)S(1)}, u32[]{:S(2)}, u32[]{:S(2)}) async-start(bf16[8,96,768]{2,1,0:T(8,128)(2,1)} %bitcast.8), calls=%async_computation.2 | async-start | bytes 2359296 | tf_op jit(solution)/shard_map/all_to_all | solution.py:95
  134.1 32.8 %collective-permute-start.1 = (bf16[576,768]{1,0:T(8,128)(2,1)}, bf16[576,768]{1,0:T(8,128)(2,1)}, u32[]{:S(2)}, u32[]{:S(2)}) collective-permute-start(bf16[576,768]{1,0:T(8,128)(2,1)} %get-tuple-element.9), channel_id=1, source_target_pairs={{0,16},{8,24},{16,0},{24,8},{1,17},{9,25},{17,1},{25,9},{2,18},{10... | collective-permute-start | bytes 2654216 | tf_op jit(solution)/shard_map/ppermute | solution.py:45
  135.6 31.3 %collective-permute-start = (bf16[576,768]{1,0:T(8,128)(2,1)}, bf16[576,768]{1,0:T(8,128)(2,1)}, u32[]{:S(2)}, u32[]{:S(2)}) collective-permute-start(bf16[576,768]{1,0:T(8,128)(2,1)} %get-tuple-element.11), channel_id=1, source_target_pairs={{0,8},{8,0},{16,24},{24,16},{1,9},{9,1},{17,25},{25,17},{2,10},{10... | collective-permute-start | bytes 2654216 | tf_op jit(solution)/shard_map/ppermute | solution.py:45
  136.2 49.7 %collective-permute-start.5 = (bf16[576,768]{1,0:T(8,128)(2,1)}, bf16[576,768]{1,0:T(8,128)(2,1)}, u32[]{:S(2)}, u32[]{:S(2)}) collective-permute-start(bf16[576,768]{1,0:T(8,128)(2,1)} %get-tuple-element.4), channel_id=1, source_target_pairs={{0,24},{8,16},{16,8},{24,0},{1,25},{9,17},{17,9},{25,1},{2,26},{10... | collective-permute-start | bytes 2654216 | tf_op jit(solution)/shard_map/ppermute | solution.py:45
  137.6 66.0 %collective-permute-start.4 = (bf16[576,768]{1,0:T(8,128)(2,1)S(1)}, bf16[576,768]{1,0:T(8,128)(2,1)}, u32[]{:S(2)}, u32[]{:S(2)}) collective-permute-start(bf16[576,768]{1,0:T(8,128)(2,1)S(1)} %get-tuple-element.5), channel_id=1, source_target_pairs={{0,16},{8,24},{16,0},{24,8},{1,17},{9,25},{17,1},{25,9},{2,18},{10... | collective-permute-start | bytes 2654216 | tf_op jit(solution)/shard_map/ppermute | solution.py:45
  148.0 55.8 %collective-permute-start.3 = (bf16[576,768]{1,0:T(8,128)(2,1)S(1)}, bf16[576,768]{1,0:T(8,128)(2,1)}, u32[]{:S(2)}, u32[]{:S(2)}) collective-permute-start(bf16[576,768]{1,0:T(8,128)(2,1)S(1)} %get-tuple-element.3), channel_id=1, source_target_pairs={{0,8},{8,0},{16,24},{24,16},{1,9},{9,1},{17,25},{25,17},{2,10},{10... | collective-permute-start | bytes 2654216 | tf_op jit(solution)/shard_map/ppermute | solution.py:45
Sparse Core Ops, SparseCore 0:
  9.9 49.9 all-gather.6
  61.7 47.2 all-gather.4
